TPU v7x, 32 devices: a whole 2x2x4 slice. The times are simulated.
32 devices in a mesh: seq: 8 (over z, x), tp: 4 (over y, core).
Axes of the slice: x: 2, y: 2, z: 4, core: 2. Of those that a mesh axis runs over, the one named last changes fastest.
Arguments:
- queries: bfloat16 [40, 1536], P(None, 'tp'), may hold values from -6 to 6
- new_keys: bfloat16 [40, 512], P('seq', 'tp'), may hold values from -12 to 12
- new_values: bfloat16 [40, 512], P('seq', 'tp'), may hold values from -6 to 6
- key_cache: bfloat16 [65536, 512], P('seq', 'tp'), may hold values from -64 to 64
- value_cache: bfloat16 [65536, 512], P('seq', 'tp'), may hold values from -6 to 6
- out_weight: bfloat16 [1536, 1536], P('tp'), may hold values from -0.75 to 0.75
- group_ids: int32 [8], replicated, may hold values from 0 to 2, as said below
- prefix_len: int32 [3], replicated, may hold values from 2560 to 10240, as said below
- suffix_len: int32 [8], replicated, may hold values from 1536 to 6144, as said below
Outputs:
- attended: bfloat16 [40, 1536], P('seq', 'tp')
Inputs may be any that keep to these rules, and one draw needn't show every extreme that they name: `group_ids`: non-decreasing; every prompt is used by 2 to 4 requests. `prefix_len`: some prompt has exactly 10240 positions. `suffix_len`: some request has exactly 6144 own positions.
All inputs are finite; a program needn't handle non-finite values.
Results may differ from a plain program's by a relative error of at most 0.011.
Values sent between devices are 32-bit elements; how exact they have to be, the bound alone decides.
A program may use at most 64 MiB of HBM per device.

v0:
```python
import jax
import jax.numpy as jnp
from jax import lax
from jax.sharding import PartitionSpec as P

HD = 64
NEW = 5


fill_score = -1e30


def segment_starts(group_ids, prefix_len, suffix_len):
    groups = jnp.arange(prefix_len.shape[0], dtype=jnp.int32)
    prefix_excl = jnp.cumsum(prefix_len) - prefix_len
    suffix_excl = jnp.cumsum(suffix_len) - suffix_len
    earlier = group_ids[None, :] < groups[:, None]
    prompt_start = prefix_excl + jnp.sum(jnp.where(earlier, suffix_len[None, :], 0), axis=1)
    member = group_ids[:, None] == groups[None, :]
    req_prompt_start = jnp.sum(jnp.where(member, prompt_start[None, :], 0), axis=1)
    req_prompt_len = jnp.sum(jnp.where(member, prefix_len[None, :], 0), axis=1)
    prefix_incl = jnp.sum(jnp.where(member, (prefix_excl + prefix_len)[None, :], 0), axis=1)
    own_start = prefix_incl + suffix_excl
    group_suffix = jnp.sum(jnp.where(member, suffix_len[:, None], 0), axis=0)
    group_end = prompt_start + prefix_len + group_suffix
    req_group_end = jnp.sum(jnp.where(member, group_end[None, :], 0), axis=1)
    return (req_prompt_start, req_prompt_len, own_start, req_group_end)


def per_device(
    queries,
    new_keys,
    new_values,
    key_cache,
    value_cache,
    out_weight,
    group_ids,
    prefix_len,
    suffix_len,
):
    rows = queries.shape[0]
    heads_local = queries.shape[1] // HD
    kv_local = key_cache.shape[1] // HD
    repeat = heads_local // kv_local
    requests = rows // NEW
    window = min(requests, 32)
    block = key_cache.shape[0]
    step_len = 1024
    prompt_start, prompt_len, own_start, group_end = segment_starts(
        group_ids, prefix_len, suffix_len
    )
    offset = lax.axis_index("seq") * block
    query_all = queries.reshape(requests, NEW, kv_local, repeat, HD)
    first_req = jnp.sum((group_end <= offset).astype(jnp.int32))
    low = jnp.minimum(first_req, requests - window)
    query_win = lax.dynamic_slice_in_dim(query_all, low, window, 0)
    pstart_win = lax.dynamic_slice_in_dim(prompt_start, low, window, 0)
    pend_win = pstart_win + lax.dynamic_slice_in_dim(prompt_len, low, window, 0)
    ostart_win = lax.dynamic_slice_in_dim(own_start, low, window, 0)
    oend_win = ostart_win + lax.dynamic_slice_in_dim(suffix_len, low, window, 0)

    def key_step(turn, carry):
        row_max, total, summed = carry
        start = turn * step_len
        keys = lax.dynamic_slice_in_dim(key_cache, start, step_len, 0).reshape(
            step_len, kv_local, HD
        )
        vals = lax.dynamic_slice_in_dim(value_cache, start, step_len, 0).reshape(
            step_len, kv_local, HD
        )
        places = offset + start + jnp.arange(step_len, dtype=jnp.int32)
        in_prompt = (places[None, :] >= pstart_win[:, None]) & (places[None, :] < pend_win[:, None])
        in_own = (places[None, :] >= ostart_win[:, None]) & (places[None, :] < oend_win[:, None])
        mask = (in_prompt | in_own)[:, None, None, None, :]
        score = (
            jnp.einsum("rtgjd,kgd->rtgjk", query_win, keys, preferred_element_type=jnp.float32)
            * 0.125
        )
        block_max = jnp.max(jnp.where(mask, score, fill_score), axis=-1)
        new_max = jnp.maximum(row_max, block_max)
        expo = jnp.where(mask, jnp.exp(score - new_max[..., None]), 0.0)
        factor = jnp.exp(row_max - new_max)
        total = total * factor + jnp.sum(expo, axis=-1)
        summed = summed * factor[..., None] + jnp.einsum(
            "rtgjk,kgd->rtgjd", expo.astype(jnp.bfloat16), vals, preferred_element_type=jnp.float32
        )
        return (new_max, total, summed)

    shape_win = (window, NEW, kv_local, repeat)
    start_state = (
        jnp.full(shape_win, fill_score, jnp.float32),
        jnp.zeros(shape_win, jnp.float32),
        jnp.zeros(shape_win + (HD,), jnp.float32),
    )
    win_max, win_total, win_summed = lax.fori_loop(0, block // step_len, key_step, start_state)
    shape_stat = (requests, NEW, kv_local, repeat)
    row_max = lax.dynamic_update_slice_in_dim(
        jnp.full(shape_stat, fill_score, jnp.float32), win_max, low, 0
    )
    total = lax.dynamic_update_slice_in_dim(jnp.zeros(shape_stat, jnp.float32), win_total, low, 0)
    summed = lax.dynamic_update_slice_in_dim(
        jnp.zeros(shape_stat + (HD,), jnp.float32), win_summed, low, 0
    )
    mine = lax.axis_index("seq")
    maxes, totals, sums = (
        lax.all_to_all(row_max, "seq", split_axis=0, concat_axis=0, tiled=True),
        lax.all_to_all(total, "seq", split_axis=0, concat_axis=0, tiled=True),
        lax.all_to_all(summed, "seq", split_axis=0, concat_axis=0, tiled=True),
    )
    own_max = jnp.max(maxes, axis=0)
    rescale = jnp.exp(maxes - own_max[None])
    own_total = jnp.sum(totals * rescale, axis=0)
    own_summed = jnp.sum(sums * rescale[..., None], axis=0)
    own_query = lax.dynamic_slice_in_dim(query_all, mine, 1, 0)[0]
    keys_new = new_keys.reshape(NEW, kv_local, HD)
    values_new = new_values.reshape(NEW, kv_local, HD)
    causal = (jnp.arange(NEW)[:, None] >= jnp.arange(NEW)[None, :])[:, None, None, :]
    score_new = (
        jnp.einsum("tgjd,ugd->tgju", own_query, keys_new, preferred_element_type=jnp.float32)
        * 0.125
    )
    joined = jnp.maximum(own_max, jnp.max(jnp.where(causal, score_new, fill_score), axis=-1))
    expo_new = jnp.where(causal, jnp.exp(score_new - joined[..., None]), 0.0)
    factor_own = jnp.exp(own_max - joined)
    denominator = own_total * factor_own + jnp.sum(expo_new, axis=-1)
    numerator = own_summed * factor_own[..., None] + jnp.einsum(
        "tgju,ugd->tgjd",
        expo_new.astype(jnp.bfloat16),
        values_new,
        preferred_element_type=jnp.float32,
    )
    mixed = (numerator / denominator[..., None]).astype(jnp.bfloat16).reshape(NEW, heads_local * HD)
    partial_out = jnp.dot(mixed, out_weight, preferred_element_type=jnp.float32)
    return lax.psum_scatter(partial_out, "tp", scatter_dimension=1, tiled=True).astype(jnp.bfloat16)


def solution(mesh):
    placed = (
        P(None, "tp"),
        P("seq", "tp"),
        P("seq", "tp"),
        P("seq", "tp"),
        P("seq", "tp"),
        P("tp", None),
        P(),
        P(),
        P(),
    )
    return jax.shard_map(
        per_device, mesh=mesh, in_specs=placed, out_specs=P("seq", "tp"), check_vma=False
    )
```

profile of v0, /device:TPU:0, one launch (start us, length us, event | category | flops | bytes accessed | tf_op | source)
XLA Modules:
  0.0 95.8 jit_solution(15413522517144196104)
XLA Ops:
  6.5 0.9 reduce-window.17
  7.5 0.8 reduce-window.18
  8.3 0.8 select_reduce_fusion.4
  9.1 0.9 reshape.227
  10.0 0.7 subtract_add_fusion
  10.6 0.8 select_reduce_fusion.1
  11.4 0.7 fusion.24
  12.1 21.1 %while.18 = (s32[]{:T(128)}, f32[8,5,2,3]{0,3,1,2:T(4,128)S(1)}, f32[8,5,2,3]{0,3,1,2:T(4,128)S(1)}, f32[8,5,2,3,64]{4,0,3,1,2:T(8,128)S(1)}, s32[]{:T(128)}, /*...) while((s32[]{:T(128)}, f32[8,5,2,3]{0,3,1,2:T(4,128)S(1)}, ...), condition=%wide.region_9.10_spmd.clone, body=%wide.region_6.9_spmd.clone.sunk | while | flops 65232056 | bytes 5780843 | solution.py:95
  12.2 1.1 %constant_dynamic-slice_fusion.4 = (bf16[1024,128]{1,0:T(8,128)(2,1)S(1)}, bf16[1024,128]{1,0:T(8,128)(2,1)S(1)}) fusion(bf16[8192,128]{1,0:T(8,128)(2,1)} %get-tuple-element.489, s32[]{:T(128)S(6)} %select_n.94, bf16[8192,128]{1,0:T(8,128)(2,1)} %get-tuple-element.487), kind=kLoop, calls=%fused_computation.18.clone.1 | loop fusion | bytes 1048580 | tf_op jit(solution)/shard_map/while/body/eval_jaxpr/dynamic_slice | solution.py:68
  13.6 0.4 select_reduce_fusion.6
  14.0 0.3 fusion.43
  14.3 0.4 fusion.45
  14.8 1.1 %constant_dynamic-slice_fusion.4 = (bf16[1024,128]{1,0:T(8,128)(2,1)S(1)}, bf16[1024,128]{1,0:T(8,128)(2,1)S(1)}) fusion(bf16[8192,128]{1,0:T(8,128)(2,1)} %get-tuple-element.489, s32[]{:T(128)S(6)} %select_n.94, bf16[8192,128]{1,0:T(8,128)(2,1)} %get-tuple-element.487), kind=kLoop, calls=%fused_computation.18.clone.1 | loop fusion | bytes 1048580 | tf_op jit(solution)/shard_map/while/body/eval_jaxpr/dynamic_slice | solution.py:68
  16.2 0.4 select_reduce_fusion.6
  16.6 0.3 fusion.43
  16.9 0.4 fusion.45
  17.5 1.1 %constant_dynamic-slice_fusion.4 = (bf16[1024,128]{1,0:T(8,128)(2,1)S(1)}, bf16[1024,128]{1,0:T(8,128)(2,1)S(1)}) fusion(bf16[8192,128]{1,0:T(8,128)(2,1)} %get-tuple-element.489, s32[]{:T(128)S(6)} %select_n.94, bf16[8192,128]{1,0:T(8,128)(2,1)} %get-tuple-element.487), kind=kLoop, calls=%fused_computation.18.clone.1 | loop fusion | bytes 1048580 | tf_op jit(solution)/shard_map/while/body/eval_jaxpr/dynamic_slice | solution.py:68
  18.8 0.4 select_reduce_fusion.6
  19.6 0.4 fusion.45
  20.1 1.1 %constant_dynamic-slice_fusion.4 = (bf16[1024,128]{1,0:T(8,128)(2,1)S(1)}, bf16[1024,128]{1,0:T(8,128)(2,1)S(1)}) fusion(bf16[8192,128]{1,0:T(8,128)(2,1)} %get-tuple-element.489, s32[]{:T(128)S(6)} %select_n.94, bf16[8192,128]{1,0:T(8,128)(2,1)} %get-tuple-element.487), kind=kLoop, calls=%fused_computation.18.clone.1 | loop fusion | bytes 1048580 | tf_op jit(solution)/shard_map/while/body/eval_jaxpr/dynamic_slice | solution.py:68
  21.5 0.4 select_reduce_fusion.6
  22.2 0.4 fusion.45
  22.7 1.1 %constant_dynamic-slice_fusion.4 = (bf16[1024,128]{1,0:T(8,128)(2,1)S(1)}, bf16[1024,128]{1,0:T(8,128)(2,1)S(1)}) fusion(bf16[8192,128]{1,0:T(8,128)(2,1)} %get-tuple-element.489, s32[]{:T(128)S(6)} %select_n.94, bf16[8192,128]{1,0:T(8,128)(2,1)} %get-tuple-element.487), kind=kLoop, calls=%fused_computation.18.clone.1 | loop fusion | bytes 1048580 | tf_op jit(solution)/shard_map/while/body/eval_jaxpr/dynamic_slice | solution.py:68
  24.1 0.4 select_reduce_fusion.6
  24.8 0.4 fusion.45
  25.4 1.1 %constant_dynamic-slice_fusion.4 = (bf16[1024,128]{1,0:T(8,128)(2,1)S(1)}, bf16[1024,128]{1,0:T(8,128)(2,1)S(1)}) fusion(bf16[8192,128]{1,0:T(8,128)(2,1)} %get-tuple-element.489, s32[]{:T(128)S(6)} %select_n.94, bf16[8192,128]{1,0:T(8,128)(2,1)} %get-tuple-element.487), kind=kLoop, calls=%fused_computation.18.clone.1 | loop fusion | bytes 1048580 | tf_op jit(solution)/shard_map/while/body/eval_jaxpr/dynamic_slice | solution.py:68
  26.7 0.4 select_reduce_fusion.6
  27.5 0.4 fusion.45
  28.0 1.1 %constant_dynamic-slice_fusion.4 = (bf16[1024,128]{1,0:T(8,128)(2,1)S(1)}, bf16[1024,128]{1,0:T(8,128)(2,1)S(1)}) fusion(bf16[8192,128]{1,0:T(8,128)(2,1)} %get-tuple-element.489, s32[]{:T(128)S(6)} %select_n.94, bf16[8192,128]{1,0:T(8,128)(2,1)} %get-tuple-element.487), kind=kLoop, calls=%fused_computation.18.clone.1 | loop fusion | bytes 1048580 | tf_op jit(solution)/shard_map/while/body/eval_jaxpr/dynamic_slice | solution.py:68
  29.4 0.4 select_reduce_fusion.6
  30.1 0.4 fusion.45
  30.6 1.1 %constant_dynamic-slice_fusion.4 = (bf16[1024,128]{1,0:T(8,128)(2,1)S(1)}, bf16[1024,128]{1,0:T(8,128)(2,1)S(1)}) fusion(bf16[8192,128]{1,0:T(8,128)(2,1)} %get-tuple-element.489, s32[]{:T(128)S(6)} %select_n.94, bf16[8192,128]{1,0:T(8,128)(2,1)} %get-tuple-element.487), kind=kLoop, calls=%fused_computation.18.clone.1 | loop fusion | bytes 1048580 | tf_op jit(solution)/shard_map/while/body/eval_jaxpr/dynamic_slice | solution.py:68
  32.0 0.4 select_reduce_fusion.6
  32.7 0.4 fusion.45
  33.1 0.7 copy.92
  33.8 7.2 %all-to-all-start.1 = ((f32[8,5,2,3]{1,2,3,0:T(2,128)}), f32[8,5,2,3]{1,2,3,0:T(2,128)S(1)}, u32[]{:S(2)}, u32[]{:S(2)}) async-start(f32[8,5,2,3]{1,2,3,0:T(2,128)} %copy.92), calls=%async_computation.1 | async-start | bytes 49152 | tf_op jit(solution)/shard_map/all_to_all | solution.py:106
  41.9 0.8 reshape.237
  42.6 0.7 copy.107
  43.4 4.4 %all-to-all-done.1 = f32[8,5,2,3]{1,2,3,0:T(2,128)S(1)} async-done(((f32[8,5,2,3]{1,2,3,0:T(2,128)}), f32[8,5,2,3]{1,2,3,0:T(2,128)S(1)}, u32[]{:S(2)}, u32[]{:S(2)}) %all-to-all-start.1) | async-done | bytes 992 | tf_op jit(solution)/shard_map/all_to_all | solution.py:106
  47.7 3.3 %all-to-all-start.2 = ((f32[8,5,2,3]{1,2,3,0:T(2,128)}), f32[8,5,2,3]{1,2,3,0:T(2,128)S(1)}, u32[]{:S(2)}, u32[]{:S(2)}) async-start(f32[8,5,2,3]{1,2,3,0:T(2,128)} %copy.107), calls=%async_computation.2 | async-start | bytes 49152 | tf_op jit(solution)/shard_map/all_to_all | solution.py:107
  51.6 6.0 %all-to-all-done.2 = f32[8,5,2,3]{1,2,3,0:T(2,128)S(1)} async-done(((f32[8,5,2,3]{1,2,3,0:T(2,128)}), f32[8,5,2,3]{1,2,3,0:T(2,128)S(1)}, u32[]{:S(2)}, u32[]{:S(2)}) %all-to-all-start.2) | async-done | bytes 992 | tf_op jit(solution)/shard_map/all_to_all | solution.py:107
  57.6 3.3 %all-to-all-start = ((f32[8,1,1920]{2,1,0:T(1,128)}), f32[8,1,1920]{2,1,0:T(1,128)S(1)}, u32[]{:S(2)}, u32[]{:S(2)}) async-start(f32[8,1,1920]{2,1,0:T(1,128)} %reshape.237), calls=%async_computation | async-start | bytes 122880 | tf_op jit(solution)/shard_map/all_to_all | solution.py:108
  61.7 6.1 %all-to-all-done = f32[8,1,1920]{2,1,0:T(1,128)S(1)} async-done(((f32[8,1,1920]{2,1,0:T(1,128)}), f32[8,1,1920]{2,1,0:T(1,128)S(1)}, u32[]{:S(2)}, u32[]{:S(2)}) %all-to-all-start) | async-done | bytes 61472 | tf_op jit(solution)/shard_map/all_to_all | solution.py:108
  67.8 0.5 broadcast.144
  68.3 0.8 reduce
  69.7 0.9 fusion.26
  70.6 17.1 %reduce-scatter.2.cloned.1.call-done = f32[5,384]{1,0:T(8,128)} async-done(((f32[5,1536]{1,0:T(8,128)}), f32[5,384]{1,0:T(8,128)}) %reduce-scatter.2.cloned.1.call-update) | async-done | bytes 7696 | tf_op jit(solution)/shard_map/reduce_scatter | solution.py:134
  87.7 1.3 %convert_element_type.19 = bf16[5,384]{1,0:T(8,128)(2,1)} convert(f32[5,384]{1,0:T(8,128)} %reduce-scatter.2.cloned.1.call-done) | non-fusion elementwise | flops 1920 | bytes 11520 | tf_op jit(solution)/shard_map/convert_element_type | solution.py:134
  (101 shorter events, 8.0 us)
Async XLA Ops:
  6.5 63.2 %copy-start = (bf16[384,1536]{1,0:T(8,128)(2,1)S(1)}, bf16[384,1536]{1,0:T(8,128)(2,1)}, u32[]{:S(2)}) copy-start(bf16[384,1536]{1,0:T(8,128)(2,1)} %param.16) | copy-start | bytes 3538948
  12.1 29.0 %copy-start.1 = (bf16[5,128]{1,0:T(8,128)(2,1)S(1)}, bf16[5,128]{1,0:T(8,128)(2,1)}, u32[]{:S(2)}) copy-start(bf16[5,128]{1,0:T(8,128)(2,1)} %param.12) | copy-start | bytes 3844
  12.1 29.5 %copy-start.2 = (bf16[5,128]{1,0:T(8,128)(2,1)S(1)}, bf16[5,128]{1,0:T(8,128)(2,1)}, u32[]{:S(2)}) copy-start(bf16[5,128]{1,0:T(8,128)(2,1)} %param.13) | copy-start | bytes 3844
  33.8 13.9 %all-to-all-start.1 = ((f32[8,5,2,3]{1,2,3,0:T(2,128)}), f32[8,5,2,3]{1,2,3,0:T(2,128)S(1)}, u32[]{:S(2)}, u32[]{:S(2)}) async-start(f32[8,5,2,3]{1,2,3,0:T(2,128)} %copy.92), calls=%async_computation.1 | async-start | bytes 49152 | tf_op jit(solution)/shard_map/all_to_all | solution.py:106
  47.7 9.9 %all-to-all-start.2 = ((f32[8,5,2,3]{1,2,3,0:T(2,128)}), f32[8,5,2,3]{1,2,3,0:T(2,128)S(1)}, u32[]{:S(2)}, u32[]{:S(2)}) async-start(f32[8,5,2,3]{1,2,3,0:T(2,128)} %copy.107), calls=%async_computation.2 | async-start | bytes 49152 | tf_op jit(solution)/shard_map/all_to_all | solution.py:107
  57.6 10.2 %all-to-all-start = ((f32[8,1,1920]{2,1,0:T(1,128)}), f32[8,1,1920]{2,1,0:T(1,128)S(1)}, u32[]{:S(2)}, u32[]{:S(2)}) async-start(f32[8,1,1920]{2,1,0:T(1,128)} %reshape.237), calls=%async_computation | async-start | bytes 122880 | tf_op jit(solution)/shard_map/all_to_all | solution.py:108
  61.0 26.7 %reduce-scatter.2.cloned.1.call-start = ((), (), s32[]{:S(2)}) async-start(), calls=%async_computation.4 | async-start | bytes 61440 | tf_op jit(solution)/shard_map/reduce_scatter | solution.py:134
Sparse Core Ops, SparseCore 0:
  70.7 16.9 reduce-scatter.1
where the time goes:
time: 96.5 us; the launch traced here: 95.8 us
  waiting for transfers between devices  33.5 us (35%)
  local copies, waits for them, and re-layouts  16.2 us (17%)
  starting transfers between devices  14 us (15%)
  between operations  13.5 us (14%)
  other arithmetic  11 us (11%)
  matrix products  7.01 us (7%)
    reduce_scatter x1, waiting for transfers between devices, per_device(): lax.psum_scatter(partial_out, 'tp', scatter_dimension=1, tiled=True)  17.1 us
    dynamic_slice x16, local copies, waits for them, and re-layouts, key_step(): lax.dynamic_slice_in_dim(value_cache, start, step_len, 0)  9.74 us
    all_to_all x1, starting transfers between devices, per_device(): lax.all_to_all(row_max, 'seq', split_axis=0, concat_axis=0, tiled=True)  7.25 us
    all_to_all x1, waiting for transfers between devices, per_device(): lax.all_to_all(summed, 'seq', split_axis=0, concat_axis=0, tiled=True)  6.1 us
    all_to_all x1, waiting for transfers between devices, per_device(): lax.all_to_all(total, 'seq', split_axis=0, concat_axis=0, tiled=True)  5.99 us
    all_to_all x1, waiting for transfers between devices, per_device(): lax.all_to_all(row_max, 'seq', split_axis=0, concat_axis=0, tiled=True)  4.35 us
    all_to_all x1, starting transfers between devices, per_device(): lax.all_to_all(summed, 'seq', split_axis=0, concat_axis=0, tiled=True)  3.35 us
    all_to_all x1, starting transfers between devices, per_device(): lax.all_to_all(total, 'seq', split_axis=0, concat_axis=0, tiled=True)  3.34 us
  transfers between devices with their start and end apart: 4, of which 4 were waited for; matrix products, arithmetic and copies ran while one was open for 4% of the time, Pallas kernels for 0%

commit v1 on v0

v1 whole, which is shorter than its diff:
```python
import functools

import jax
import jax.numpy as jnp
from jax import lax
from jax.experimental import pallas as pl
from jax.experimental.pallas import tpu as pltpu
from jax.sharding import PartitionSpec as P

HD = 64
NEW = 5
CHUNK = 1024
ROWS_REQ = 32
HALF = 16
MASKED = -1e30
FLOOR = -1e29
MESH = pl.DeviceIdType.MESH


def nt_dot(a, b):
    return lax.dot_general(a, b, (((1,), (1,)), ((), ())), preferred_element_type=jnp.float32)


def pack_halves(x, lane_low):
    parts = []
    for i in range(x.shape[0] // ROWS_REQ):
        first = x[i * ROWS_REQ : i * ROWS_REQ + HALF]
        second = x[i * ROWS_REQ + HALF : (i + 1) * ROWS_REQ]
        parts.append(jnp.where(lane_low, first, second))
    return parts[0] if len(parts) == 1 else jnp.concatenate(parts, axis=0)


def kernel(
    n_seq,
    n_tp,
    window,
    gid_ref,
    plen_ref,
    slen_ref,
    q_ref,
    nk_ref,
    nv_ref,
    k_hbm,
    v_hbm,
    w_hbm,
    out_ref,
    kbuf,
    vbuf,
    wbuf,
    qbuf,
    newbuf,
    mbuf,
    lbuf,
    abuf,
    sendbuf,
    recvbuf,
    mixbuf,
    psend,
    precv,
    k_sem,
    v_sem,
    w_sem,
    send_sem,
    recv_sem,
    psend_sem,
    precv_sem,
):
    me = lax.axis_index("seq")
    mine = lax.axis_index("tp")
    requests = gid_ref.shape[0]
    groups = plen_ref.shape[0]
    block = kbuf.shape[0]
    chunks = block // CHUNK
    heads = q_ref.shape[1] // HD
    rep = heads // 2

    k_copies, v_copies = [], []
    for c in range(chunks):
        rows = pl.ds(c * CHUNK, CHUNK)
        kc = pltpu.make_async_copy(k_hbm.at[rows], kbuf.at[rows], k_sem.at[c])
        vc = pltpu.make_async_copy(v_hbm.at[rows], vbuf.at[rows], v_sem.at[c])
        kc.start()
        vc.start()
        k_copies.append(kc)
        v_copies.append(vc)
    w_copies = []
    for j in range(rep):
        for g in range(2):
            wc = pltpu.make_async_copy(
                w_hbm.at[pl.ds((g * rep + j) * HD, HD)],
                wbuf.at[pl.ds((j * 2 + g) * HD, HD)],
                w_sem.at[j * 2 + g],
            )
            wc.start()
            w_copies.append(wc)

    barrier = pltpu.get_barrier_semaphore()
    for k in range(1, n_seq):
        pl.semaphore_signal(
            barrier, inc=1, device_id={"seq": lax.rem(me + k, n_seq)}, device_id_type=MESH
        )
    for k in range(1, n_tp):
        pl.semaphore_signal(
            barrier, inc=1, device_id={"tp": lax.rem(mine + k, n_tp)}, device_id_type=MESH
        )

    run = jnp.int32(0)
    base = jnp.int32(0)
    before = None
    spans = []
    for r in range(requests):
        g = gid_ref[r]
        if r > 0:
            base = jnp.where(g != before, run, base)
        before = g
        earlier = jnp.int32(0)
        here = jnp.int32(0)
        for i in range(groups):
            length = plen_ref[i]
            earlier = earlier + jnp.where(g > i, length, 0)
            here = jnp.where(g == i, length, here)
        own = slen_ref[r]
        spans.append((earlier + base, here, earlier + here + run, own))
        run = run + own

    span = 8 * NEW
    row = lax.broadcasted_iota(jnp.int32, (8 * ROWS_REQ, span), 0)
    col = lax.broadcasted_iota(jnp.int32, (8 * ROWS_REQ, span), 1)
    place = row & (HALF - 1)
    rrep = sum((place >= NEW * j).astype(jnp.int32) for j in range(1, rep))
    head = ((row >> 4) & 1) * rep + rrep
    match = (col == (row >> 5) * NEW + place - NEW * rrep) & (place < rep * NEW)
    same = (head & 1) == ((row >> 4) & 1)
    lane = lax.broadcasted_iota(jnp.int32, (8 * ROWS_REQ, 2 * HD), 1)
    group_row = (lax.broadcasted_iota(jnp.int32, (8 * ROWS_REQ, 2 * HD), 0) >> 4) & 1
    in_group = (lane >= HD).astype(jnp.int32) == group_row
    straight = []
    crossed = []
    for tile in range(heads // 2):
        at = match & ((head >> 1) == tile)
        straight.append((at & same).astype(jnp.float32).astype(jnp.bfloat16))
        crossed.append((at & ~same).astype(jnp.float32).astype(jnp.bfloat16))
    q_all = q_ref[...]
    for i in range(requests // 8):
        keep = jnp.zeros((8 * ROWS_REQ, 2 * HD), jnp.float32)
        turn = jnp.zeros((8 * ROWS_REQ, 2 * HD), jnp.float32)
        for tile in range(heads // 2):
            piece = q_all[i * span : (i + 1) * span, tile * 2 * HD : (tile + 1) * 2 * HD]
            keep += jnp.dot(straight[tile], piece, preferred_element_type=jnp.float32)
            turn += jnp.dot(crossed[tile], piece, preferred_element_type=jnp.float32)
        both = (keep + pltpu.roll(turn, HD, 1)) * 0.125
        both = jnp.where(in_group, both, 0.0)
        qbuf[pl.ds(i * 8 * ROWS_REQ, 8 * ROWS_REQ), :] = both.astype(jnp.bfloat16)

    lane_low = lax.broadcasted_iota(jnp.int32, (HALF, 2 * HD), 1) < HD

    newbuf[...] = jnp.zeros_like(newbuf)
    newbuf[0, 0:NEW, :] = nk_ref[...].astype(jnp.float32)
    newbuf[1, 0:NEW, :] = nv_ref[...].astype(jnp.float32)
    q_own = qbuf[pl.ds(pl.multiple_of(me * ROWS_REQ, ROWS_REQ), ROWS_REQ), :]
    s_new = nt_dot(q_own, newbuf[0].astype(jnp.bfloat16))
    place_n = lax.broadcasted_iota(jnp.int32, s_new.shape, 0) & (HALF - 1)
    token_n = place_n - sum(
        (place_n >= NEW * j).astype(jnp.int32) * NEW for j in range(1, rep + 1)
    )
    causal = lax.broadcasted_iota(jnp.int32, s_new.shape, 1) <= token_n
    s_new = jnp.where(causal, s_new, MASKED)
    m_new = jnp.max(s_new, axis=1, keepdims=True)
    p_new = jnp.exp(s_new - m_new)
    l_new = jnp.sum(p_new, axis=1, keepdims=True)
    a_new = jnp.dot(
        p_new.astype(jnp.bfloat16),
        newbuf[1].astype(jnp.bfloat16),
        preferred_element_type=jnp.float32,
    )
    o_new = pack_halves(a_new / l_new, lane_low)
    stat_new = pack_halves(m_new + jnp.log(l_new), lane_low)

    offset = me * block
    wpad = -(-window // 8) * 8
    slot = lax.broadcasted_iota(jnp.int32, (wpad, 128), 0)
    pos = lax.broadcasted_iota(jnp.int32, (wpad, CHUNK), 1)
    bounds = []
    for f in range(4):
        vec = jnp.zeros((wpad, 128), jnp.int32)
        for i in range(window):
            vec = jnp.where(slot == i, spans[i][f], vec)
        bounds.append(vec[:, 0:1])
    for c in range(chunks):
        start = offset + c * CHUNK
        shifted = pos + start
        from_p = shifted - bounds[0]
        from_o = shifted - bounds[2]
        live = ((from_p >= 0) & (from_p < bounds[1])) | ((from_o >= 0) & (from_o < bounds[3]))
        bias = jnp.where(live, 0.0, MASKED)

        k_copies[c].wait()
        s = nt_dot(qbuf[...], kbuf[pl.ds(c * CHUNK, CHUNK), :])
        ps, ms, ls = [], [], []
        for i in range(window):
            si = s[i * ROWS_REQ : (i + 1) * ROWS_REQ] + bias[i : i + 1, :]
            mi = jnp.maximum(jnp.max(si, axis=1, keepdims=True), FLOOR)
            pi = jnp.exp(si - mi)
            ls.append(jnp.sum(pi, axis=1, keepdims=True))
            ms.append(mi)
            ps.append(pi.astype(jnp.bfloat16))
        v_copies[c].wait()
        acc = jnp.dot(
            jnp.concatenate(ps, axis=0),
            vbuf[pl.ds(c * CHUNK, CHUNK), :],
            preferred_element_type=jnp.float32,
        )
        abuf[c] = pack_halves(acc, lane_low)
        for i in range(window):
            at = pl.ds(i * HALF, HALF)
            mbuf[c, at, :] = pack_halves(ms[i], lane_low)
            lbuf[c, at, :] = pack_halves(ls[i], lane_low)

    def merged(r):
        tops, sums, accs = [], [], []
        for c in range(chunks):
            at = pl.ds(pl.multiple_of(r * HALF, HALF), HALF)
            tops.append(mbuf[c, at, :])
            sums.append(lbuf[c, at, :])
            accs.append(abuf[c, at, :])
        top = functools.reduce(jnp.maximum, tops, jnp.full((HALF, 2 * HD), FLOOR, jnp.float32))
        total = jnp.zeros((HALF, 2 * HD), jnp.float32)
        summed = jnp.zeros((HALF, 2 * HD), jnp.float32)
        for m, l, a in zip(tops, sums, accs):
            w = jnp.exp(m - top)
            total += w * l
            summed += w * a
        some = total > 0.0
        safe = jnp.where(some, total, 1.0)
        return summed / safe, jnp.where(some, top + jnp.log(safe), MASKED)

    pl.semaphore_wait(barrier, n_seq - 1 + n_tp - 1)

    def seq_copy(k):
        return pltpu.make_async_remote_copy(
            src_ref=sendbuf.at[k],
            dst_ref=recvbuf.at[k],
            send_sem=send_sem.at[k],
            recv_sem=recv_sem.at[k],
            device_id={"seq": lax.rem(me + k, n_seq)},
            device_id_type=MESH,
        )

    def send_part(k, carry):
        o, stat = merged(lax.rem(me + k, n_seq))
        sendbuf[k, 0:HALF, :] = o
        sendbuf[k, HALF : 2 * HALF, :] = stat
        seq_copy(k).start()
        return carry

    if n_seq <= 8:
        for k in range(1, n_seq):
            send_part(k, 0)
    else:
        lax.fori_loop(1, n_seq, send_part, 0)

    o_here, stat_here = merged(me)

    def take(carry, o, stat):
        top, total, summed = carry
        higher = jnp.maximum(top, stat)
        a, b = jnp.exp(top - higher), jnp.exp(stat - higher)
        return higher, total * a + b, summed * a + o * b

    carry = (stat_new, jnp.ones_like(stat_new), o_new)
    carry = take(carry, o_here, stat_here)
    if n_seq <= 8:
        for k in range(1, n_seq):
            seq_copy(k).wait_recv()
        stats = [recvbuf[k, HALF : 2 * HALF, :] for k in range(1, n_seq)]
        top = functools.reduce(jnp.maximum, stats, carry[0])
        fac = jnp.exp(carry[0] - top)
        total, summed = carry[1] * fac, carry[2] * fac
        for k in range(1, n_seq):
            w = jnp.exp(stats[k - 1] - top)
            total += w
            summed += w * recvbuf[k, 0:HALF, :]
    else:

        def take_part(k, carry):
            seq_copy(k).wait_recv()
            return take(carry, recvbuf[k, 0:HALF, :], recvbuf[k, HALF : 2 * HALF, :])

        _, total, summed = lax.fori_loop(1, n_seq, take_part, carry)
    mixbuf[...] = jnp.zeros_like(mixbuf)
    mixbuf[0:HALF, :] = summed / total
    lhs = jnp.concatenate([mixbuf[pl.ds(NEW * j, 8), :] for j in range(rep)], axis=1)
    lhs = lhs.astype(jnp.bfloat16)
    for wc in w_copies:
        wc.wait()
    partial = jnp.dot(lhs, wbuf[...], preferred_element_type=jnp.float32)
    width = psend.shape[2]
    for i in range(n_tp):
        psend[i] = partial[:, i * width : (i + 1) * width]
    copies = []
    for k in range(1, n_tp):
        dest = lax.rem(mine + k, n_tp)
        pc = pltpu.make_async_remote_copy(
            src_ref=psend.at[dest],
            dst_ref=precv.at[k],
            send_sem=psend_sem.at[k],
            recv_sem=precv_sem.at[k],
            device_id={"tp": dest},
            device_id_type=MESH,
        )
        pc.start()
        copies.append(pc)
    result = psend[mine]
    for k, pc in enumerate(copies, 1):
        pc.wait_recv()
        result = result + precv[k]
    out_ref[...] = result[0:NEW].astype(jnp.bfloat16)
    for pc in copies:
        pc.wait_send()
    if n_seq <= 8:
        for k in range(1, n_seq):
            seq_copy(k).wait_send()
    else:

        def finish(k, carry):
            seq_copy(k).wait_send()
            return carry

        lax.fori_loop(1, n_seq, finish, 0)


def solution(mesh):
    n_seq, n_tp = mesh.shape["seq"], mesh.shape["tp"]

    def per_device(q, nk, nv, kc, vc, w, gid, plen, slen):
        requests, groups = gid.shape[0], plen.shape[0]
        block = kc.shape[0]
        chunks = block // CHUNK
        window = requests
        width = w.shape[1] // n_tp
        smem = pl.BlockSpec(memory_space=pltpu.SMEM)
        vmem = pl.BlockSpec(memory_space=pltpu.VMEM)
        hbm = pl.BlockSpec(memory_space=pl.ANY)
        f32, bf16 = jnp.float32, jnp.bfloat16
        dma = pltpu.SemaphoreType.DMA
        return pl.pallas_call(
            functools.partial(kernel, n_seq, n_tp, window),
            out_shape=jax.ShapeDtypeStruct((NEW, width), bf16),
            in_specs=[smem] * 3 + [vmem] * 3 + [hbm] * 3,
            out_specs=vmem,
            scratch_shapes=[
                pltpu.VMEM((block, 2 * HD), bf16),
                pltpu.VMEM((block, 2 * HD), bf16),
                pltpu.VMEM(w.shape, bf16),
                pltpu.VMEM((requests * ROWS_REQ, 2 * HD), bf16),
                pltpu.VMEM((2, HALF, 2 * HD), f32),
                pltpu.VMEM((chunks, window * HALF, 2 * HD), f32),
                pltpu.VMEM((chunks, window * HALF, 2 * HD), f32),
                pltpu.VMEM((chunks, window * HALF, 2 * HD), f32),
                pltpu.VMEM((n_seq, 2 * HALF, 2 * HD), f32),
                pltpu.VMEM((n_seq, 2 * HALF, 2 * HD), f32),
                pltpu.VMEM((24, 2 * HD), f32),
                pltpu.VMEM((n_tp, 8, width), f32),
                pltpu.VMEM((n_tp, 8, width), f32),
                dma((chunks,)),
                dma((chunks,)),
                dma((w.shape[0] // HD,)),
                dma((n_seq,)),
                dma((n_seq,)),
                dma((n_tp,)),
                dma((n_tp,)),
            ],
            compiler_params=pltpu.CompilerParams(
                collective_id=0, has_side_effects=True, vmem_limit_bytes=48 * 1024 * 1024
            ),
            name="attend",
        )(gid, plen, slen, q, nk, nv, kc, vc, w)

    placed = (
        P(None, "tp"),
        P("seq", "tp"),
        P("seq", "tp"),
        P("seq", "tp"),
        P("seq", "tp"),
        P("tp", None),
        P(),
        P(),
        P(),
    )
    return jax.shard_map(
        per_device, mesh=mesh, in_specs=placed, out_specs=P("seq", "tp"), check_vma=False
    )
```

time: 96.5 us -> 31.3 us (0.32)
  waiting for transfers between devices: 33.5 us -> 0 us
  Pallas kernels: 0 us -> 21.8 us
  starting transfers between devices: 14 us -> 0 us
  between operations: 13.5 us -> 0.02 us
  other arithmetic: 11 us -> 0 us
  local copies, waits for them, and re-layouts: 16.2 us -> 9.13 us
  matrix products: 7.01 us -> 0 us
    pallas_call x0 -> x1, Pallas kernels: none -> 21.8 us  [per_device(): pl.pallas_call(functools.partial(kernel, n_seq, n_tp, window), out_shape=...]
    reduce_scatter x1 -> x0, waiting for transfers between devices: 17.1 us -> none  [per_device(): lax.psum_scatter(partial_out, 'tp', scatter_dimension=1, tiled=True)]
    all_to_all x3 -> x0, waiting for transfers between devices: 16.4 us -> none  [the longest x1 6.1 us: per_device(): lax.all_to_all(summed, 'seq', split_axis=0, concat_axis=0, tiled=True)]
    all_to_all x3 -> x0, starting transfers between devices: 13.9 us -> none  [the longest x1 7.25 us: per_device(): lax.all_to_all(row_max, 'seq', split_axis=0, concat_axis=0, tiled=True)]
    dynamic_slice x25 -> x0, local copies, waits for them, and re-layouts: 10.9 us -> none  [the longest x16 9.74 us: key_step(): lax.dynamic_slice_in_dim(value_cache, start, step_len, 0)]
    unnamed x12 -> x19, local copies, waits for them, and re-layouts: 1.24 us -> 9.13 us
    dot_general x19 -> x0, matrix products: 7.01 us -> none  [the longest x8 2.97 us: key_step(): jnp.einsum('rtgjk,kgd->rtgjd', expo.astype(jnp.bfloat16), vals, preferred...]
    reduce_sum x13 -> x0, other arithmetic: 4.56 us -> none  [the longest x8 2.57 us: key_step(): total = total * factor + jnp.sum(expo, axis=-1)]
  transfers between devices with their start and end apart: 4 -> 0, of which waited for: 4 -> 0; matrix products, arithmetic and copies ran while one was open for 4% -> 0% of each run, Pallas kernels for 0% -> 0%
where the time goes in v1:
time: 31.3 us; the launch traced here: 31 us
  Pallas kernels  21.8 us (70%)
  local copies, waits for them, and re-layouts  9.13 us (29%)
    pallas_call x1, Pallas kernels, per_device(): pl.pallas_call(functools.partial(kernel, n_seq, n_tp, window), out_shape=...  21.8 us
    unnamed x19, local copies, waits for them, and re-layouts  9.13 us

profile of v1, /device:TPU:0, one launch (start us, length us, event | category | flops | bytes accessed | tf_op | source)
XLA Modules:
  0.0 31.0 jit_solution(5899643472884386045)
XLA Ops:
  0.0 0.0 copy-start
  0.0 1.6 %copy-done = bf16[8192,128]{1,0:T(8,128)(2,1)S(1)} copy-done((bf16[8192,128]{1,0:T(8,128)(2,1)S(1)}, bf16[8192,128]{1,0:T(8,128)(2,1)}, u32[]{:S(2)}) %copy-start) | copy-done | bytes 2097176
  1.6 0.0 copy-start.1
  1.6 1.6 %copy-done.1 = bf16[8192,128]{1,0:T(8,128)(2,1)S(1)} copy-done((bf16[8192,128]{1,0:T(8,128)(2,1)S(1)}, bf16[8192,128]{1,0:T(8,128)(2,1)}, u32[]{:S(2)}) %copy-start.1) | copy-done | bytes 2097176
  3.2 0.0 copy-start.2
  3.2 1.3 %copy-done.2 = bf16[384,1536]{1,0:T(8,128)(2,1)S(1)} copy-done((bf16[384,1536]{1,0:T(8,128)(2,1)S(1)}, bf16[384,1536]{1,0:T(8,128)(2,1)}, u32[]{:S(2)}) %copy-start.2) | copy-done | bytes 1179672
  4.5 0.0 copy-start.3
  4.5 0.8 %copy-done.3 = bf16[40,384]{1,0:T(8,128)(2,1)S(1)} copy-done((bf16[40,384]{1,0:T(8,128)(2,1)S(1)}, bf16[40,384]{1,0:T(8,128)(2,1)}, u32[]{:S(2)}) %copy-start.3) | copy-done | bytes 30744
  5.2 0.0 copy-start.4
  5.2 0.7 %copy-done.4 = bf16[5,128]{1,0:T(8,128)(2,1)S(1)} copy-done((bf16[5,128]{1,0:T(8,128)(2,1)S(1)}, bf16[5,128]{1,0:T(8,128)(2,1)}, u32[]{:S(2)}) %copy-start.4) | copy-done | bytes 1304
  5.9 0.0 copy-start.5
  5.9 0.7 %copy-done.5 = bf16[5,128]{1,0:T(8,128)(2,1)S(1)} copy-done((bf16[5,128]{1,0:T(8,128)(2,1)S(1)}, bf16[5,128]{1,0:T(8,128)(2,1)}, u32[]{:S(2)}) %copy-start.5) | copy-done | bytes 1304
  6.6 0.0 copy-start.6
  6.6 0.7 %copy-done.6 = s32[8]{0:T(128)S(1)} copy-done((s32[8]{0:T(128)S(1)}, s32[8]{0:T(128)}, u32[]{:S(2)}) %copy-start.6) | copy-done | bytes 56
  7.2 0.0 copy-start.7
  7.2 0.7 %copy-done.7 = s32[3]{0:T(128)S(1)} copy-done((s32[3]{0:T(128)S(1)}, s32[3]{0:T(128)}, u32[]{:S(2)}) %copy-start.7) | copy-done | bytes 36
  7.9 0.0 copy-start.8
  7.9 0.7 %copy-done.8 = s32[8]{0:T(128)S(1)} copy-done((s32[8]{0:T(128)S(1)}, s32[8]{0:T(128)}, u32[]{:S(2)}) %copy-start.8) | copy-done | bytes 56
  8.5 21.8 %attend.1 = bf16[5,384]{1,0:T(8,128)(2,1)S(1)} custom-call(s32[8]{0:T(128)S(1)} %copy-done.6, s32[3]{0:T(128)S(1)} %copy-done.7, s32[8]{0:T(128)S(1)} %copy-done.8, bf16[40,384]{1,0:T(8,128)(2,1)S(1)} %copy-done.3, bf16[5,128]{1,0:T(8,128)(2,1)S(1)} %copy-done.4, bf16[5,128]{1,0:T(8,128)(2,1)S(1)} %copy-done.5, bf16[8192,128]{1,0:T(8,128)(2,1)S(1)} %copy-done, ...), custom_call_target="tpu_custom_call" | custom-call | tf_op jit(solution)/shard_map/attend/pallas_call | solution.py:346
  30.4 0.6 %copy.11 = bf16[5,384]{1,0:T(8,128)(2,1)} copy(bf16[5,384]{1,0:T(8,128)(2,1)S(1)} %attend.1) | data formatting | bytes 7680
Async XLA Ops:
  0.0 1.6 %copy-start = (bf16[8192,128]{1,0:T(8,128)(2,1)S(1)}, bf16[8192,128]{1,0:T(8,128)(2,1)}, u32[]{:S(2)}) copy-start(bf16[8192,128]{1,0:T(8,128)(2,1)} %k_hbm.1) | copy-start | bytes 6291460
  1.6 1.6 %copy-start.1 = (bf16[8192,128]{1,0:T(8,128)(2,1)S(1)}, bf16[8192,128]{1,0:T(8,128)(2,1)}, u32[]{:S(2)}) copy-start(bf16[8192,128]{1,0:T(8,128)(2,1)} %v_hbm.1) | copy-start | bytes 6291460
  3.2 1.3 %copy-start.2 = (bf16[384,1536]{1,0:T(8,128)(2,1)S(1)}, bf16[384,1536]{1,0:T(8,128)(2,1)}, u32[]{:S(2)}) copy-start(bf16[384,1536]{1,0:T(8,128)(2,1)} %w_hbm.1) | copy-start | bytes 3538948
  4.5 0.8 %copy-start.3 = (bf16[40,384]{1,0:T(8,128)(2,1)S(1)}, bf16[40,384]{1,0:T(8,128)(2,1)}, u32[]{:S(2)}) copy-start(bf16[40,384]{1,0:T(8,128)(2,1)} %q_ref.1) | copy-start | bytes 92164
  5.2 0.7 %copy-start.4 = (bf16[5,128]{1,0:T(8,128)(2,1)S(1)}, bf16[5,128]{1,0:T(8,128)(2,1)}, u32[]{:S(2)}) copy-start(bf16[5,128]{1,0:T(8,128)(2,1)} %nk_ref.1) | copy-start | bytes 3844
  5.9 0.7 %copy-start.5 = (bf16[5,128]{1,0:T(8,128)(2,1)S(1)}, bf16[5,128]{1,0:T(8,128)(2,1)}, u32[]{:S(2)}) copy-start(bf16[5,128]{1,0:T(8,128)(2,1)} %nv_ref.1) | copy-start | bytes 3844
  6.6 0.7 %copy-start.6 = (s32[8]{0:T(128)S(1)}, s32[8]{0:T(128)}, u32[]{:S(2)}) copy-start(s32[8]{0:T(128)} %gid_ref.1) | copy-start | bytes 100
  7.2 0.7 %copy-start.7 = (s32[3]{0:T(128)S(1)}, s32[3]{0:T(128)}, u32[]{:S(2)}) copy-start(s32[3]{0:T(128)} %plen_ref.1) | copy-start | bytes 40
  7.9 0.7 %copy-start.8 = (s32[8]{0:T(128)S(1)}, s32[8]{0:T(128)}, u32[]{:S(2)}) copy-start(s32[8]{0:T(128)} %slen_ref.1) | copy-start | bytes 100
